TPU v7x, 32 devices: a whole 2x2x4 slice. The times are simulated.
32 devices in a mesh: pipe: 2 (over y), expert: 4 (over z), tensor: 4 (over x, core).
Axes of the slice: x: 2, y: 2, z: 4, core: 2. Of those that a mesh axis runs over, the one named last changes fastest.
Arguments:
- stream: bfloat16 [1024, 6144], P(('pipe', 'expert'), 'tensor')
- norm_gain: float32 [6144], P('tensor'), may hold values from 0.5 to 1.5
- attn_gain: float32 [6144], P('tensor'), may hold values from 0.5 to 1.5
- router: float32 [6144, 4], P('tensor'), may hold values from -0.078125 to 0.078125
- expert_ids: int32 [1024, 2], P(('pipe', 'expert')), may hold values from 0 to 3, as said below
- expert_slots: int32 [1024, 2], P(('pipe', 'expert')), may hold values from -1 to 39, as said below
- w_gate: bfloat16 [4, 6144, 8192], P('expert', None, ('pipe', 'tensor')), may hold values from -0.078125 to 0.078125
- w_up: bfloat16 [4, 6144, 8192], P('expert', None, ('pipe', 'tensor')), may hold values from -0.078125 to 0.078125
- w_down: bfloat16 [4, 8192, 6144], P('expert', ('pipe', 'tensor')), may hold values from -0.09375 to 0.09375
- w_query: bfloat16 [6144, 6144], P('tensor', ('pipe', 'expert'))
- w_key: bfloat16 [6144, 1024], P('tensor')
- w_value: bfloat16 [6144, 1024], P('tensor'), may hold values from -0.078125 to 0.078125
Outputs:
- new_stream: bfloat16 [1024, 6144], P(('pipe', 'expert'), 'tensor')
- attended: bfloat16 [1024, 6144], P('tensor', ('pipe', 'expert'))
Inputs may be any that keep to these rules, and one draw needn't show every extreme that they name: `expert_ids`: each row names two different experts. `expert_slots`: within the rows of one group of 128 tokens, each expert's picks take slots 0, 1, 2 and so on in token order (pick 0 before pick 1) until 40 are taken, later picks of that expert are -1; so each pair of expert and slot is named at most once in a group.
All inputs are finite; a program needn't handle non-finite values.
Results may differ from a plain program's by a relative error of at most 0.015.
Values may be sent and summed in bfloat16 or wider, within the bound.
A program may use at most 128 MiB of HBM per device.

v0:
```python
import math

import jax
import jax.numpy as jnp
from jax import lax
from jax.sharding import PartitionSpec as P

D = 6144
QH = 48
KVH = 8
HD = 128
CAP = 40


NORM_EPS = 1e-05


def expert_block(expert_rows, gate_weight, up_weight, down_weight):
    shard_piece = lax.all_gather(expert_rows, "tensor", axis=1, tiled=True)
    gate_total = jnp.dot(shard_piece, gate_weight, preferred_element_type=jnp.float32)
    up_total = jnp.dot(shard_piece, up_weight, preferred_element_type=jnp.float32)
    hidden_value = (jax.nn.silu(gate_total) * up_total).astype(jnp.bfloat16)
    partial_out = jnp.dot(hidden_value, down_weight, preferred_element_type=jnp.float32)
    return lax.psum_scatter(partial_out, "tensor", scatter_dimension=1, tiled=True)


def on_device(
    stream,
    norm_gain,
    attn_gain,
    router,
    expert_ids,
    expert_slots,
    w_gate,
    w_up,
    w_down,
    w_query,
    w_key,
    w_value,
):
    token_rows, local_width = stream.shape
    experts = router.shape[1]
    stream_f = stream.astype(jnp.float32)
    scaled = stream_f * norm_gain
    square_part = jnp.sum(stream_f * stream_f, axis=1)
    logit_part = jnp.dot(scaled, router, precision=lax.Precision.HIGHEST)
    squares, logit_sum = lax.psum((square_part, logit_part), "tensor")
    inverse = lax.rsqrt(squares / D + NORM_EPS)
    normed = (scaled * inverse[:, None]).astype(jnp.bfloat16)
    logits = inverse[:, None] * logit_sum
    onehot = expert_ids[:, :, None] == jnp.arange(experts, dtype=jnp.int32)[None, None, :]
    picked = jnp.sum(jnp.where(onehot, logits[:, None, :], 0.0), axis=2)
    first_share = jax.nn.sigmoid(picked[:, 0] - picked[:, 1])
    mixing = jnp.stack([first_share, 1.0 - first_share], axis=1)
    slot_total = experts * CAP
    target = jnp.where(expert_slots >= 0, expert_ids * CAP + expert_slots, slot_total)
    copies = jnp.broadcast_to(normed[:, None, :], (token_rows, 2, local_width)).reshape(
        token_rows * 2, local_width
    )
    outgoing = (
        jnp.zeros((slot_total + 1, local_width), jnp.bfloat16)
        .at[target.reshape(-1)]
        .set(copies)[:slot_total]
    )
    arrived = lax.all_to_all(outgoing, "expert", split_axis=0, concat_axis=0, tiled=True)
    both_halves = lax.all_gather(arrived, "pipe", axis=0, tiled=True)
    half_sums = expert_block(both_halves, w_gate[0], w_up[0], w_down[0])
    summed = lax.psum_scatter(half_sums, "pipe", scatter_dimension=0, tiled=True)
    expert_out = summed.astype(jnp.bfloat16)
    returned = lax.all_to_all(expert_out, "expert", split_axis=0, concat_axis=0, tiled=True)
    padded = jnp.concatenate([returned, jnp.zeros((1, local_width), jnp.bfloat16)], axis=0)
    picked_rows = padded[target].astype(jnp.float32)
    moe_sum = mixing[:, 0:1] * picked_rows[:, 0] + mixing[:, 1:2] * picked_rows[:, 1]
    new_stream = (stream_f + moe_sum).astype(jnp.bfloat16)
    attn_f = new_stream.astype(jnp.float32)
    square_two = lax.psum(jnp.sum(attn_f * attn_f, axis=1), "tensor")
    attn_in = (attn_f * lax.rsqrt(square_two / D + NORM_EPS)[:, None] * attn_gain).astype(
        jnp.bfloat16
    )
    head_group = lax.axis_index(("pipe", "expert"))
    query_width = w_query.shape[1]
    heads_here = query_width // HD
    shared_head = head_group * heads_here // (QH // KVH)
    key_columns = lax.dynamic_slice_in_dim(w_key, shared_head * HD, HD, 1)
    value_columns = lax.dynamic_slice_in_dim(w_value, shared_head * HD, HD, 1)
    projector = jnp.concatenate([w_query, key_columns, value_columns], axis=1)
    partial_proj = jnp.dot(
        lax.all_gather(attn_in, ("pipe", "expert"), axis=0, tiled=True),
        projector,
        preferred_element_type=jnp.float32,
    )
    own_proj = lax.psum_scatter(partial_proj, "tensor", scatter_dimension=0, tiled=True)
    query_rows = own_proj.shape[0]
    queries = own_proj[:, :query_width].astype(jnp.bfloat16).reshape(query_rows, heads_here, HD)
    key_rows = own_proj[:, query_width : query_width + HD].astype(jnp.bfloat16)
    value_rows = own_proj[:, query_width + HD :].astype(jnp.bfloat16)
    first_row = lax.axis_index("tensor") * query_rows
    query_pos = first_row + jnp.arange(query_rows, dtype=jnp.int32)
    score_scale = 1.0 / math.sqrt(HD)
    best = jnp.full((heads_here, query_rows), -1e30, jnp.float32)
    key_piece = lax.all_gather(key_rows, "tensor", axis=0, tiled=True)
    value_piece = lax.all_gather(value_rows, "tensor", axis=0, tiled=True)
    key_pos = jnp.arange(key_piece.shape[0], dtype=jnp.int32)
    allowed = (key_pos[None, :] <= query_pos[:, None])[None, :, :]
    scores = (
        jnp.einsum("qhd,kd->hqk", queries, key_piece, preferred_element_type=jnp.float32)
        * score_scale
    )
    scores = jnp.where(allowed, scores, -1e30)
    new_best = jnp.maximum(best, jnp.max(scores, axis=2))
    weights = jnp.where(allowed, jnp.exp(scores - new_best[:, :, None]), 0.0)
    total = jnp.sum(weights, axis=2)
    update = jnp.einsum(
        "hqk,kd->hqd", weights.astype(jnp.bfloat16), value_piece, preferred_element_type=jnp.float32
    )
    accum = update
    best, total, accum = (new_best, total, accum)
    context = accum / total[:, :, None]
    attended = context.transpose(1, 0, 2).reshape(query_rows, query_width).astype(jnp.bfloat16)
    return (new_stream, attended)


def solution(mesh):
    in_specs = (
        P(("pipe", "expert"), "tensor"),
        P("tensor"),
        P("tensor"),
        P("tensor", None),
        P(("pipe", "expert"), None),
        P(("pipe", "expert"), None),
        P("expert", None, ("pipe", "tensor")),
        P("expert", None, ("pipe", "tensor")),
        P("expert", ("pipe", "tensor"), None),
        P("tensor", ("pipe", "expert")),
        P("tensor", None),
        P("tensor", None),
    )
    out_specs = (P(("pipe", "expert"), "tensor"), P("tensor", ("pipe", "expert")))
    return jax.shard_map(
        on_device, mesh=mesh, in_specs=in_specs, out_specs=out_specs, check_vma=False
    )
```

profile of v0, /device:TPU:0, one launch (start us, length us, event | category | flops | bytes accessed | tf_op | source)
XLA Modules:
  0.0 383.5 jit_solution(11872580938256117115)
XLA Ops:
  7.2 0.0 all-gather.3.cloned.1.call-start
  7.2 0.7 compare_select_fusion.1
  7.9 0.1 copy.33
  8.0 0.1 reshape.81
  8.2 1.2 fusion.45
  9.4 1.7 fusion.40
  11.1 8.3 %all-reduce.1 = (f32[128]{0:T(128)S(1)}, f32[128,4]{0,1:T(4,128)S(1)}) all-reduce(f32[128]{0:T(128)S(1)} %fusion.45, f32[128,4]{0,1:T(4,128)S(1)} %fusion.40), channel_id=1, replica_groups=mesh['pipe'=2,'expert'=4,'tensor'=4] {'tensor'}, use_global_device_ids=true, to_apply=%region_1.0 | all-reduce | flops 640 | bytes 5120 | tf_op jit(solution)/shard_map/psum | solution.py:47
  19.4 1.1 fusion.41
  20.5 0.4 broadcast_in_dim.68
  20.9 0.3 reshape.96
  21.2 1.9 scatter_custom_fusion
  23.2 17.3 %all_to_all.24 = bf16[4,40,1536]{2,1,0:T(8,128)(2,1)S(1)} all-to-all(bf16[4,40,1536]{2,1,0:T(8,128)(2,1)S(1)} %bitcast.79), channel_id=1, replica_groups=mesh['pipe'=2,'expert'=4,'tensor'=4] {'expert'}, dimensions={0} | all-to-all | bytes 983040 | tf_op jit(solution)/shard_map/all_to_all | solution.py:65
  40.4 12.1 %all_gather.15 = bf16[320,1536]{1,0:T(8,128)(2,1)} all-gather(bf16[160,1536]{1,0:T(8,128)(2,1)S(1)} %bitcast.80), channel_id=1, replica_groups=mesh['pipe'=2,'expert'=4,'tensor'=4] {'pipe'}, dimensions={0}, use_global_device_ids=true | all-gather | bytes 1474560 | tf_op jit(solution)/shard_map/all_gather | solution.py:66
  52.5 0.0 all-gather.3.cloned.1.call-update
  52.6 0.0 reduce-scatter.4.cloned.1.call-start
  52.6 33.4 %all-gather.3.cloned.1.call-done = bf16[320,6144]{1,0:T(8,128)(2,1)} async-done(((bf16[320,1536]{1,0:T(8,128)(2,1)}), bf16[320,6144]{1,0:T(8,128)(2,1)}) %all-gather.3.cloned.1.call-update) | async-done | bytes 3932176 | tf_op jit(solution)/shard_map/all_gather | solution.py:19
  86.0 8.5 %fusion.4 = f32[320,1024]{1,0:T(8,128)S(1)} fusion(bf16[320,6144]{1,0:T(8,128)(2,1)} %all-gather.3.cloned.1.call-done, bf16[1,6144,1024]{2,1,0:T(8,128)(2,1)} %param.18), kind=kOutput, calls=%fused_computation.6 | convolution fusion | flops 4026531840 | bytes 17825792 | tf_op jit(solution)/shard_map/dot_general | solution.py:20
  94.5 20.8 %fusion = f32[320,6144]{1,0:T(8,128)} fusion(bf16[1,1024,6144]{2,1,0:T(8,128)(2,1)} %param.20, bf16[320,6144]{1,0:T(8,128)(2,1)} %all-gather.3.cloned.1.call-done, bf16[1,6144,1024]{2,1,0:T(8,128)(2,1)} %param.19, f32[320,1024]{1,0:T(8,128)S(1)} %fusion.4), kind=kOutput, calls=%fused_computation.2 | convolution fusion | flops 8055029760 | bytes 38273024 | tf_op jit(solution)/shard_map/dot_general | solution.py:23
  115.3 0.0 reduce-scatter.4.cloned.1.call-update
  115.4 0.0 reduce-scatter.6.cloned.1.call-start
  115.4 69.1 %reduce-scatter.4.cloned.1.call-done = f32[320,1536]{1,0:T(8,128)} async-done(((f32[320,6144]{1,0:T(8,128)}), f32[320,1536]{1,0:T(8,128)}) %reduce-scatter.4.cloned.1.call-update) | async-done | bytes 1966096 | tf_op jit(solution)/shard_map/reduce_scatter | solution.py:24
  184.5 32.8 %reduce-scatter.6.cloned.1.call-done = f32[160,1536]{1,0:T(8,128)} async-done(((f32[320,1536]{1,0:T(8,128)}), f32[160,1536]{1,0:T(8,128)}) %reduce-scatter.6.cloned.1.call-update) | async-done | bytes 983056 | tf_op jit(solution)/shard_map/reduce_scatter | solution.py:68
  217.3 2.0 convert_element_type.39
  219.4 4.6 %all-to-all-start.1 = ((bf16[4,40,1536]{2,1,0:T(8,128)(2,1)}), bf16[4,40,1536]{2,1,0:T(8,128)(2,1)S(1)}, u32[]{:S(2)}, u32[]{:S(2)}) async-start(bf16[4,40,1536]{2,1,0:T(8,128)(2,1)} %bitcast.7), calls=%async_computation.3 | async-start | bytes 983040 | tf_op jit(solution)/shard_map/all_to_all | solution.py:70
  224.0 0.1 copy.34
  224.1 0.1 reshape.86
  224.3 13.5 %all-to-all-done.1 = bf16[4,40,1536]{2,1,0:T(8,128)(2,1)S(1)} async-done(((bf16[4,40,1536]{2,1,0:T(8,128)(2,1)}), bf16[4,40,1536]{2,1,0:T(8,128)(2,1)S(1)}, u32[]{:S(2)}, u32[]{:S(2)}) %all-to-all-start.1) | async-done | bytes 491552 | tf_op jit(solution)/shard_map/all_to_all | solution.py:70
  237.8 1.3 gather_fusion
  239.1 1.0 reshape.102
  240.0 1.2 fusion.63
  241.3 0.3 fusion.42
  241.6 5.8 %psum.23 = f32[128]{0:T(128)S(1)} all-reduce(f32[128]{0:T(128)S(1)} %get-tuple-element.10), channel_id=1, replica_groups=mesh['pipe'=2,'expert'=4,'tensor'=4] {'tensor'}, use_global_device_ids=true, to_apply=%region_8.9 | all-reduce | flops 128 | bytes 1024 | tf_op jit(solution)/shard_map/psum | solution.py:76
  247.4 0.9 fusion.44
  248.3 0.0 reduce-scatter.8.cloned.1.call-start
  248.4 1.2 constant_dynamic-slice_fusion
  249.6 57.6 %all-gather.5.cloned.1.call-done = bf16[1024,1536]{1,0:T(8,128)(2,1)} async-done(((bf16[128,1536]{1,0:T(8,128)(2,1)}), bf16[1024,1536]{1,0:T(8,128)(2,1)}) %all-gather.5.cloned.1.call-update) | async-done | bytes 3145744 | tf_op jit(solution)/shard_map/all_gather | solution.py:88
  307.3 8.0 %fusion.9 = f32[1024,1024]{1,0:T(8,128)} fusion(bf16[1024,1536]{1,0:T(8,128)(2,1)} %all-gather.5.cloned.1.call-done, bf16[1536,128]{1,0:T(8,128)(2,1)S(1)} %get-tuple-element.22, bf16[1536,128]{1,0:T(8,128)(2,1)S(1)} %get-tuple-element.23, bf16[1536,768]{1,0:T(8,128)(2,1)} %param.21), kind=kOutput, calls=%fused_computation.13 | convolution fusion | flops 3230662656 | bytes 10485760 | tf_op jit(solution)/shard_map/dot_general | solution.py:87
  315.2 0.0 reduce-scatter.8.cloned.1.call-update
  315.2 0.2 iota_compare_fusion
  315.4 43.1 %reduce-scatter.8.cloned.1.call-done = f32[256,1024]{1,0:T(8,128)} async-done(((f32[1024,1024]{1,0:T(8,128)}), f32[256,1024]{1,0:T(8,128)}) %reduce-scatter.8.cloned.1.call-update) | async-done | bytes 1048592 | tf_op jit(solution)/shard_map/reduce_scatter | solution.py:92
  358.5 1.3 convert.5
  359.9 0.2 copy.37
  360.1 5.8 %all_gather.18 = bf16[1024,128]{1,0:T(8,128)(2,1)S(1)} all-gather(bf16[256,128]{1,0:T(8,128)(2,1)S(1)} %get-tuple-element.19), channel_id=1, replica_groups=mesh['pipe'=2,'expert'=4,'tensor'=4] {'tensor'}, dimensions={0}, use_global_device_ids=true | all-gather | bytes 327680 | tf_op jit(solution)/shard_map/all_gather | solution.py:101
  365.9 1.1 fusion.6
  367.0 5.9 %all_gather.19 = bf16[1024,128]{1,0:T(8,128)(2,1)S(1)} all-gather(bf16[256,128]{1,0:T(8,128)(2,1)S(1)} %get-tuple-element.18), channel_id=1, replica_groups=mesh['pipe'=2,'expert'=4,'tensor'=4] {'tensor'}, dimensions={0}, use_global_device_ids=true | all-gather | bytes 327680 | tf_op jit(solution)/shard_map/all_gather | solution.py:102
  372.8 1.5 fusion.7
  374.4 1.7 fusion.36
  376.1 0.9 copy.41
  (28 shorter events, 0.3 us)
Async XLA Ops:
  7.2 2.2 copy-start
  7.2 78.8 %all-gather.3.cloned.1.call-start = ((), (), s32[]{:S(2)}) async-start(), calls=%async_computation.5 | async-start | bytes 4915200 | tf_op jit(solution)/shard_map/all_gather | solution.py:19
  52.6 131.9 %reduce-scatter.4.cloned.1.call-start = ((), (), s32[]{:S(2)}) async-start(), calls=%async_computation.6 | async-start | bytes 9830400 | tf_op jit(solution)/shard_map/reduce_scatter | solution.py:24
  115.3 108.9 %copy-start.5 = (s32[128,2]{0,1:T(2,128)S(1)}, s32[128,2]{0,1:T(2,128)}, u32[]{:S(2)}) copy-start(s32[128,2]{0,1:T(2,128)} %param.16) | copy-start | bytes 3076
  115.4 101.9 %reduce-scatter.6.cloned.1.call-start = ((), (), s32[]{:S(2)}) async-start(), calls=%async_computation.7 | async-start | bytes 2949120 | tf_op jit(solution)/shard_map/reduce_scatter | solution.py:68
  219.4 18.4 %all-to-all-start.1 = ((bf16[4,40,1536]{2,1,0:T(8,128)(2,1)}), bf16[4,40,1536]{2,1,0:T(8,128)(2,1)S(1)}, u32[]{:S(2)}, u32[]{:S(2)}) async-start(bf16[4,40,1536]{2,1,0:T(8,128)(2,1)} %bitcast.7), calls=%async_computation.3 | async-start | bytes 983040 | tf_op jit(solution)/shard_map/all_to_all | solution.py:70
  223.9 83.3 %all-gather.5.cloned.1.call-start = ((), (), s32[]{:S(2)}) async-start(), calls=%async_computation.8 | async-start | bytes 3538944 | tf_op jit(solution)/shard_map/all_gather | solution.py:88
  237.8 3.5 copy-start.2
  237.8 9.6 %copy-start.4 = (f32[1536]{0:T(1024)S(1)}, f32[1536]{0:T(1024)}, u32[]{:S(2)}) copy-start(f32[1536]{0:T(1024)} %param.14) | copy-start | bytes 18436
  241.6 73.6 %copy-start.3 = (bf16[128,1536]{1,0:T(8,128)(2,1)}, bf16[128,1536]{1,0:T(8,128)(2,1)S(1)}, u32[]{:S(2)}) copy-start(bf16[128,1536]{1,0:T(8,128)(2,1)S(1)} %get-tuple-element.11) | copy-start | bytes 1179652
  248.3 110.2 %reduce-scatter.8.cloned.1.call-start = ((), (), s32[]{:S(2)}) async-start(), calls=%async_computation.9 | async-start | bytes 5242880 | tf_op jit(solution)/shard_map/reduce_scatter | solution.py:92
  374.4 2.6 copy-start.1
Sparse Core Ops, SparseCore 0:
  52.7 33.3 all-gather.2
  115.5 68.9 reduce-scatter.3
  186.8 30.4 reduce-scatter.5
  248.5 58.7 all-gather.4
  315.4 43.1 reduce-scatter.7
where the time goes:
time: 384 us
  waiting for transfers between devices  250 us (65%)
  blocking collectives  55.1 us (14%)
  matrix products  41.8 us (11%)
  between operations  14 us (4%)
  other arithmetic  9.31 us (2%)
  local copies, waits for them, and re-layouts  8.99 us (2%)
  starting transfers between devices  4.76 us (1%)
    reduce_scatter x1, waiting for transfers between devices, expert_block(): lax.psum_scatter(partial_out, 'tensor', scatter_dimension=1, tiled=True)  69.1 us
    all_gather x1, waiting for transfers between devices, on_device(): lax.all_gather(attn_in, ('pipe', 'expert'), axis=0, tiled=True)  57.6 us
    reduce_scatter x1, waiting for transfers between devices, on_device(): lax.psum_scatter(partial_proj, 'tensor', scatter_dimension=0, tiled=True)  43.1 us
    all_gather x1, waiting for transfers between devices, expert_block(): shard_piece = lax.all_gather(expert_rows, 'tensor', axis=1, tiled=True)  33.4 us
    reduce_scatter x1, waiting for transfers between devices, on_device(): lax.psum_scatter(half_sums, 'pipe', scatter_dimension=0, tiled=True)  32.8 us
    dot_general x1, matrix products, expert_block(): jnp.dot(hidden_value, down_weight, preferred_element_type=jnp.float32)  20.8 us
    all_to_all x1, blocking collectives, on_device(): lax.all_to_all(outgoing, 'expert', split_axis=0, concat_axis=0, tiled=True)  17.3 us
    all_to_all x1, waiting for transfers between devices, on_device(): lax.all_to_all(expert_out, 'expert', split_axis=0, concat_axis=0, tiled=T...  13.5 us
  transfers between devices with their start and end apart: 6, of which 6 were waited for; matrix products, arithmetic and copies ran while one was open for 0% of the time, Pallas kernels for 0%

commit v1 on v0

--- a/solution.py
+++ b/solution.py
@@ -1,8 +1,11 @@
+import functools
 import math
 
 import jax
 import jax.numpy as jnp
 from jax import lax
+from jax.experimental import pallas as pl
+from jax.experimental.pallas import tpu as pltpu
 from jax.sharding import PartitionSpec as P
 
 D = 6144
@@ -10,18 +13,249 @@
 KVH = 8
 HD = 128
 CAP = 40
-
-
 NORM_EPS = 1e-05
-
-
-def expert_block(expert_rows, gate_weight, up_weight, down_weight):
-    shard_piece = lax.all_gather(expert_rows, "tensor", axis=1, tiled=True)
-    gate_total = jnp.dot(shard_piece, gate_weight, preferred_element_type=jnp.float32)
-    up_total = jnp.dot(shard_piece, up_weight, preferred_element_type=jnp.float32)
-    hidden_value = (jax.nn.silu(gate_total) * up_total).astype(jnp.bfloat16)
-    partial_out = jnp.dot(hidden_value, down_weight, preferred_element_type=jnp.float32)
-    return lax.psum_scatter(partial_out, "tensor", scatter_dimension=1, tiled=True)
+MESH = pl.DeviceIdType.MESH
+MIB = 1024 * 1024
+
+
+def lane_tile(width):
+    return 256 if width % 256 == 0 else 128
+
+
+def expert_kernel(
+    np_, ne, nt, out_ref_shape, going, wg_hbm, wu_hbm, wd_hbm, back,
+    rows, wg, wu, wd, lhs, acc_g, acc_u, hid, part, sib_out, sib_in, tgt_out, tgt_in, zbuf,
+    w_sem, own_sem, zs, zr, cs, cr, ss, sr, bs, br, ts, tr, rs, rr,
+):
+    nc = nt // 2
+    p = lax.axis_index("pipe")
+    e = lax.axis_index("expert")
+    t = lax.axis_index("tensor")
+    c, k = t // 2, t % 2
+    width = going.shape[2]
+    hidden = wg.shape[2]
+    count = np_ * ne * CAP
+    sib = (p, e, c * 2 + (1 - k))
+
+    def chip(dc, dp):
+        return (lax.rem(p + dp, np_), e, lax.rem(c + dc, nc) * 2 + k)
+
+    def plane(de):
+        return (p, lax.rem(e + de, ne), t)
+
+    chips = [(dc, dp) for dc in range(nc) for dp in range(np_) if (dc, dp) != (0, 0)]
+    order = [(dc, dk) for dc in range(nc) for dk in range(2)]
+
+    own = pltpu.make_async_copy(going.at[e], rows.at[0, 0, 0, 0], own_sem)
+    own.start()
+    loads = {}
+    for j, (dc, dk) in enumerate(order):
+        piece = lax.rem(c + dc, nc) * 2 + lax.rem(k + dk, 2)
+        at = pl.ds(pl.multiple_of(piece * width, 128), width)
+        loads["g", j] = pltpu.make_async_copy(wg_hbm.at[at, :], wg.at[j], w_sem.at[0, j])
+        loads["u", j] = pltpu.make_async_copy(wu_hbm.at[at, :], wu.at[j], w_sem.at[1, j])
+        loads["d", j] = pltpu.make_async_copy(wd_hbm.at[:, at], wd.at[j], w_sem.at[2, j])
+
+    barrier = pltpu.get_barrier_semaphore()
+    peers = [sib] + [chip(dc, dp) for dc, dp in chips] + [plane(de) for de in range(1, ne)]
+    for peer in peers:
+        pl.semaphore_signal(barrier, inc=1, device_id=peer, device_id_type=MESH)
+    pl.semaphore_wait(barrier, len(peers))
+
+    def send(src, dst, s_sem, r_sem, peer):
+        copy = pltpu.make_async_remote_copy(
+            src_ref=src, dst_ref=dst, send_sem=s_sem, recv_sem=r_sem,
+            device_id=peer, device_id_type=MESH,
+        )
+        copy.start()
+        return copy
+
+    sent = []
+
+    def landed(ref, s_sem, r_sem):
+        pltpu.make_async_remote_copy(
+            src_ref=ref, dst_ref=ref, send_sem=s_sem, recv_sem=r_sem,
+            device_id=sib, device_id_type=MESH,
+        ).wait_recv()
+
+    for de in range(1, ne):
+        back_de = ne - de
+        sent.append(send(
+            going.at[lax.rem(e + de, ne)], rows.at[0, 0, 0, back_de],
+            zs.at[de], zr.at[back_de], plane(de),
+        ))
+    own.wait()
+    for j in range(nt):
+        loads["g", j].start()
+        loads["u", j].start()
+    for j in range(nt):
+        loads["d", j].start()
+
+    def to_sibling(dc, dp, de):
+        sent.append(send(
+            rows.at[dc, 0, dp, de], rows.at[dc, 1, dp, de],
+            ss.at[dc, dp, de], sr.at[dc, dp, de], sib,
+        ))
+
+    zorder = [0] + [de for d in range(1, ne) for de in sorted({d, ne - d}) if d <= ne - d]
+    for de in zorder:
+        if de:
+            landed(rows.at[0, 0, 0, de], zs.at[de], zr.at[de])
+        for dc, dp in chips:
+            oc, op = (nc - dc) % nc, (np_ - dp) % np_
+            sent.append(send(
+                rows.at[0, 0, 0, de], rows.at[oc, 0, op, de],
+                cs.at[dc, dp, de], cr.at[oc, op, de], chip(dc, dp),
+            ))
+        to_sibling(0, 0, de)
+
+    def arrivals(dc):
+        for de in zorder:
+            for dp in range(np_):
+                if (dc, dp) != (0, 0):
+                    landed(rows.at[dc, 0, dp, de], cs.at[dc, dp, de], cr.at[dc, dp, de])
+                    to_sibling(dc, dp, de)
+
+    lt = lane_tile(width)
+    ht = lane_tile(hidden)
+
+    def gate_up(j, dc, dk):
+        if dk == 1:
+            for dp in range(np_):
+                for de in range(ne):
+                    landed(rows.at[dc, 1, dp, de], ss.at[dc, dp, de], sr.at[dc, dp, de])
+
+        def flat(n, carry):
+            at = pl.ds(pl.multiple_of(n * lt, lt), lt)
+            block = rows[dc, dk, :, :, :, at].astype(jnp.float32)
+            lhs[:, at] = block.reshape(count, lt).astype(jnp.bfloat16)
+            return carry
+
+        lax.fori_loop(0, width // lt, flat, 0)
+        loads["g", j].wait()
+        loads["u", j].wait()
+
+        def tile(n, carry):
+            at = pl.ds(pl.multiple_of(n * ht, ht), ht)
+            g = jnp.dot(lhs[...], wg[j, :, at], preferred_element_type=jnp.float32)
+            u = jnp.dot(lhs[...], wu[j, :, at], preferred_element_type=jnp.float32)
+            if j:
+                g = g + acc_g[:, at]
+                u = u + acc_u[:, at]
+            if j == nt - 1:
+                hid[:, at] = (g / (1.0 + jnp.exp(-g)) * u).astype(jnp.bfloat16)
+            else:
+                acc_g[:, at] = g
+                acc_u[:, at] = u
+            return carry
+
+        lax.fori_loop(0, hidden // ht, tile, 0)
+
+    for dc in range(nc):
+        arrivals(dc)
+        for dk in range(2):
+            gate_up(dc * 2 + dk, dc, dk)
+
+    for dc in reversed(range(nc)):
+        j = dc * 2 + 1
+        loads["d", j].wait()
+
+        def sibling_tile(n, carry, j=j, dc=dc):
+            at = pl.ds(pl.multiple_of(n * lt, lt), lt)
+            y = jnp.dot(hid[...], wd[j, :, at], preferred_element_type=jnp.float32)
+            sib_out[dc, :, :, :, at] = y.reshape(np_, ne, CAP, lt).astype(jnp.bfloat16)
+            return carry
+
+        lax.fori_loop(0, width // lt, sibling_tile, 0)
+        sent.append(send(sib_out.at[dc], sib_in.at[dc], bs.at[dc], br.at[dc], sib))
+        j = dc * 2
+        loads["d", j].wait()
+
+        def own_tile(n, carry, j=j):
+            at = pl.ds(pl.multiple_of(n * lt, lt), lt)
+            y = jnp.dot(hid[...], wd[j, :, at], preferred_element_type=jnp.float32)
+            part[:, :, :, at] = y.reshape(np_, ne, CAP, lt)
+            return carry
+
+        lax.fori_loop(0, width // lt, own_tile, 0)
+        landed(sib_in.at[dc], bs.at[dc], br.at[dc])
+        for de in list(range(1, ne)) + [0]:
+            for dp in range(np_):
+                if (dc, dp) != (0, 0):
+                    tgt_out[dc, dp, de] = (
+                        part[dp, de] + sib_in[dc, dp, de].astype(jnp.float32)
+                    ).astype(jnp.bfloat16)
+                    oc, op = (nc - dc) % nc, (np_ - dp) % np_
+                    sent.append(send(
+                        tgt_out.at[dc, dp, de], tgt_in.at[oc, op, de],
+                        ts.at[dc, dp, de], tr.at[oc, op, de], chip(dc, dp),
+                    ))
+
+    for de in list(range(1, ne)) + [0]:
+        total = part[0, de] + sib_in[0, 0, de].astype(jnp.float32)
+        for dc, dp in chips:
+            landed(tgt_in.at[dc, dp, de], ts.at[dc, dp, de], tr.at[dc, dp, de])
+            total = total + tgt_in[dc, dp, de].astype(jnp.float32)
+        if de:
+            zbuf[de] = total.astype(jnp.bfloat16)
+            sent.append(send(
+                zbuf.at[de], back.at[e], rs.at[de], rr.at[ne - de], plane(de),
+            ))
+        else:
+            back[e] = total.astype(jnp.bfloat16)
+    for de in range(1, ne):
+        landed(back.at[lax.rem(e + de, ne)], rs.at[de], rr.at[de])
+    for copy in sent:
+        copy.wait_send()
+
+
+def expert_layer(going, gate, up, down, sizes):
+    np_, ne, nt = sizes
+    nc = nt // 2
+    width = going.shape[2]
+    hidden = gate.shape[1]
+    count = np_ * ne * CAP
+    dma = pltpu.SemaphoreType.DMA
+    bf, f32 = jnp.bfloat16, jnp.float32
+    vm = pl.BlockSpec(memory_space=pltpu.VMEM)
+    hbm = pl.BlockSpec(memory_space=pl.ANY)
+    return pl.pallas_call(
+        functools.partial(expert_kernel, np_, ne, nt, going.shape),
+        out_shape=jax.ShapeDtypeStruct(going.shape, bf),
+        in_specs=[vm, hbm, hbm, hbm],
+        out_specs=vm,
+        scratch_shapes=[
+            pltpu.VMEM((nc, 2, np_, ne, CAP, width), bf),
+            pltpu.VMEM((nt, width, hidden), bf),
+            pltpu.VMEM((nt, width, hidden), bf),
+            pltpu.VMEM((nt, hidden, width), bf),
+            pltpu.VMEM((count, width), bf),
+            pltpu.VMEM((count, hidden), f32),
+            pltpu.VMEM((count, hidden), f32),
+            pltpu.VMEM((count, hidden), bf),
+            pltpu.VMEM((np_, ne, CAP, width), f32),
+            pltpu.VMEM((nc, np_, ne, CAP, width), bf),
+            pltpu.VMEM((nc, np_, ne, CAP, width), bf),
+            pltpu.VMEM((nc, np_, ne, CAP, width), bf),
+            pltpu.VMEM((nc, np_, ne, CAP, width), bf),
+            pltpu.VMEM((ne, CAP, width), bf),
+            dma((3, nt)),
+            dma,
+            dma((ne,)), dma((ne,)),
+            dma((nc, np_, ne)), dma((nc, np_, ne)),
+            dma((nc, np_, ne)), dma((nc, np_, ne)),
+            dma((nc,)), dma((nc,)),
+            dma((nc, np_, ne)), dma((nc, np_, ne)),
+            dma((ne,)), dma((ne,)),
+        ],
+        compiler_params=pltpu.CompilerParams(
+            collective_id=0, has_side_effects=True, vmem_limit_bytes=62 * MIB
+        ),
+        cost_estimate=pl.CostEstimate(
+            flops=6 * count * D * hidden, bytes_accessed=6 * D * hidden, transcendentals=0
+        ),
+        name="expert_layer",
+    )(going, gate, up, down)
 
 
 def on_device(
@@ -62,12 +296,10 @@
         .at[target.reshape(-1)]
         .set(copies)[:slot_total]
     )
-    arrived = lax.all_to_all(outgoing, "expert", split_axis=0, concat_axis=0, tiled=True)
-    both_halves = lax.all_gather(arrived, "pipe", axis=0, tiled=True)
-    half_sums = expert_block(both_halves, w_gate[0], w_up[0], w_down[0])
-    summed = lax.psum_scatter(half_sums, "pipe", scatter_dimension=0, tiled=True)
-    expert_out = summed.astype(jnp.bfloat16)
-    returned = lax.all_to_all(expert_out, "expert", split_axis=0, concat_axis=0, tiled=True)
+    sizes = tuple(lax.axis_size(name) for name in ("pipe", "expert", "tensor"))
+    returned = expert_layer(
+        outgoing.reshape(experts, CAP, local_width), w_gate[0], w_up[0], w_down[0], sizes
+    ).reshape(slot_total, local_width)
     padded = jnp.concatenate([returned, jnp.zeros((1, local_width), jnp.bfloat16)], axis=0)
     picked_rows = padded[target].astype(jnp.float32)
     moe_sum = mixing[:, 0:1] * picked_rows[:, 0] + mixing[:, 1:2] * picked_rows[:, 1]

time: 384 us -> 248 us (0.65)
  waiting for transfers between devices: 250 us -> 102 us
  Pallas kernels: 0 us -> 74.1 us
  matrix products: 41.8 us -> 12.5 us
  blocking collectives: 55.1 us -> 26.1 us
  starting transfers between devices: 4.76 us -> 0.26 us
    reduce_scatter x2 -> x0, waiting for transfers between devices: 102 us -> none  [the longest x1 69.1 us: expert_block(): lax.psum_scatter(partial_out, 'tensor', scatter_dimension=1, tiled=True)]
    pallas_call x0 -> x1, Pallas kernels: none -> 74.1 us  [expert_layer(): pl.pallas_call(functools.partial(expert_kernel, np_, ne, nt, going.shape)...]
    all_gather x1 -> x0, waiting for transfers between devices: 33.4 us -> none  [expert_block(): shard_piece = lax.all_gather(expert_rows, 'tensor', axis=1, tiled=True)]
    dot_general x2 -> x0, matrix products: 29.3 us -> none  [the longest x1 20.8 us: expert_block(): jnp.dot(hidden_value, down_weight, preferred_element_type=jnp.float32)]
    all_to_all x1 -> x0, blocking collectives: 17.3 us -> none  [on_device(): lax.all_to_all(outgoing, 'expert', split_axis=0, concat_axis=0, tiled=True)]
    all_to_all x1 -> x0, waiting for transfers between devices: 13.5 us -> none  [on_device(): lax.all_to_all(expert_out, 'expert', split_axis=0, concat_axis=0, tiled=T...]
    all_gather x1 -> x0, blocking collectives: 12.1 us -> none  [on_device(): both_halves = lax.all_gather(arrived, 'pipe', axis=0, tiled=True)]
    all_to_all x1 -> x0, starting transfers between devices: 4.6 us -> none  [on_device(): lax.all_to_all(expert_out, 'expert', split_axis=0, concat_axis=0, tiled=T...]
  transfers between devices with their start and end apart: 6 -> 2, of which waited for: 6 -> 2; matrix products, arithmetic and copies ran while one was open for 0% -> 1% of each run, Pallas kernels for 0% -> 0%
where the time goes in v1:
time: 248 us; the launch traced here: 247 us
  waiting for transfers between devices  102 us (41%)
  Pallas kernels  74.1 us (30%)
  blocking collectives  26.1 us (11%)
  between operations  14.3 us (6%)
  matrix products  12.5 us (5%)
  local copies, waits for them, and re-layouts  10.8 us (4%)
  other arithmetic  7.27 us (3%)
    pallas_call x1, Pallas kernels, expert_layer(): pl.pallas_call(functools.partial(expert_kernel, np_, ne, nt, going.shape)...  74.1 us
    all_gather x1, waiting for transfers between devices, on_device(): lax.all_gather(attn_in, ('pipe', 'expert'), axis=0, tiled=True)  58.7 us
    reduce_scatter x1, waiting for transfers between devices, on_device(): lax.psum_scatter(partial_proj, 'tensor', scatter_dimension=0, tiled=True)  43.1 us
    psum x1, blocking collectives, on_device(): squares, logit_sum = lax.psum((square_part, logit_part), 'tensor')  8.33 us
    dot_general x1, matrix products, on_device(): jnp.dot(lax.all_gather(attn_in, ('pipe', 'expert'), axis=0, tiled=True),...  7.95 us
    psum x1, blocking collectives, on_device(): square_two = lax.psum(jnp.sum(attn_f * attn_f, axis=1), 'tensor')  6.14 us
    all_gather x1, blocking collectives, on_device(): value_piece = lax.all_gather(value_rows, 'tensor', axis=0, tiled=True)  5.87 us
    all_gather x1, blocking collectives, on_device(): key_piece = lax.all_gather(key_rows, 'tensor', axis=0, tiled=True)  5.79 us
  transfers between devices with their start and end apart: 2, of which 2 were waited for; matrix products, arithmetic and copies ran while one was open for 1% of the time, Pallas kernels for 0%

profile of v1, /device:TPU:0, one launch (start us, length us, event | category | flops | bytes accessed | tf_op | source)
XLA Modules:
  0.0 247.1 jit_solution(17561137114399377636)
XLA Ops:
  7.2 0.0 copy-start
  7.2 0.0 all-gather.2.cloned.1.call-start
  7.2 1.2 fusion.27
  8.4 0.0 copy-done
  8.4 1.7 fusion.22
  10.1 8.3 %all-reduce.1 = (f32[128]{0:T(128)S(1)}, f32[128,4]{0,1:T(4,128)S(1)}) all-reduce(f32[128]{0:T(128)S(1)} %fusion.27, f32[128,4]{0,1:T(4,128)S(1)} %fusion.22), channel_id=1, replica_groups=mesh['pipe'=2,'expert'=4,'tensor'=4] {'tensor'}, use_global_device_ids=true, to_apply=%region_1.0 | all-reduce | flops 640 | bytes 5120 | tf_op jit(solution)/shard_map/psum | solution.py:281
  18.4 1.1 fusion.23
  19.6 0.4 broadcast_in_dim.68
  20.0 0.3 reshape.100
  20.3 0.7 compare_select_fusion.1
  21.0 0.1 copy.33
  21.1 0.1 reshape.83
  21.2 1.9 scatter_custom_fusion
  23.1 0.8 slice.37
  23.9 74.1 %expert_layer.1 = bf16[4,40,1536]{2,1,0:T(8,128)(2,1)} custom-call(bf16[4,40,1536]{2,1,0:T(8,128)(2,1)} %bitcast.64, bf16[6144,1024]{1,0:T(8,128)(2,1)} %bitcast.69, bf16[6144,1024]{1,0:T(8,128)(2,1)} %bitcast.70, bf16[1024,6144]{1,0:T(8,128)(2,1)} %bitcast.71), custom_call_target="tpu_custom_call" | custom-call | flops 12079595520 | bytes 37748736 | tf_op jit(solution)/shard_map/expert_layer/pallas_call | solution.py:222
  98.1 1.1 concatenate.6
  99.1 0.1 copy.34
  99.3 0.1 reshape.90
  99.4 0.0 copy-start.5
  99.4 0.0 copy-start.2
  99.4 0.0 copy-start.4
  99.5 1.3 gather_fusion
  100.7 1.0 reshape.106
  101.7 1.2 fusion.43
  102.9 0.0 copy-done.5
  103.0 0.0 copy-done.2
  103.0 0.3 fusion.24
  103.3 6.1 %psum.23 = f32[128]{0:T(128)S(1)} all-reduce(f32[128]{0:T(128)S(1)} %get-tuple-element.10), channel_id=1, replica_groups=mesh['pipe'=2,'expert'=4,'tensor'=4] {'tensor'}, use_global_device_ids=true, to_apply=%region_6.7 | all-reduce | flops 128 | bytes 1024 | tf_op jit(solution)/shard_map/psum | solution.py:308
  109.5 0.0 copy-done.4
  109.5 0.9 fusion.26
  110.4 0.0 all-gather.2.cloned.1.call-update
  110.4 0.2 reduce-scatter.2.cloned.1.call-start
  110.7 1.2 constant_dynamic-slice_fusion
  111.9 58.7 %all-gather.2.cloned.1.call-done = bf16[1024,1536]{1,0:T(8,128)(2,1)} async-done(((bf16[128,1536]{1,0:T(8,128)(2,1)}), bf16[1024,1536]{1,0:T(8,128)(2,1)}) %all-gather.2.cloned.1.call-update) | async-done | bytes 3145744 | tf_op jit(solution)/shard_map/all_gather | solution.py:320
  170.6 8.0 %fusion.3 = f32[1024,1024]{1,0:T(8,128)} fusion(bf16[1024,1536]{1,0:T(8,128)(2,1)} %all-gather.2.cloned.1.call-done, bf16[1536,128]{1,0:T(8,128)(2,1)S(1)} %get-tuple-element.22, bf16[1536,128]{1,0:T(8,128)(2,1)S(1)} %get-tuple-element.23, bf16[1536,768]{1,0:T(8,128)(2,1)} %param.21), kind=kOutput, calls=%fused_computation.7 | convolution fusion | flops 3230662656 | bytes 10485760 | tf_op jit(solution)/shard_map/dot_general | solution.py:319
  178.5 0.0 copy-done.3
  178.5 0.0 reduce-scatter.2.cloned.1.call-update
  178.6 0.2 iota_compare_fusion
  178.7 43.1 %reduce-scatter.2.cloned.1.call-done = f32[256,1024]{1,0:T(8,128)} async-done(((f32[1024,1024]{1,0:T(8,128)}), f32[256,1024]{1,0:T(8,128)}) %reduce-scatter.2.cloned.1.call-update) | async-done | bytes 1048592 | tf_op jit(solution)/shard_map/reduce_scatter | solution.py:324
  221.8 1.3 convert.5
  223.2 0.2 copy.37
  223.4 5.8 %all_gather.10 = bf16[1024,128]{1,0:T(8,128)(2,1)S(1)} all-gather(bf16[256,128]{1,0:T(8,128)(2,1)S(1)} %get-tuple-element.19), channel_id=1, replica_groups=mesh['pipe'=2,'expert'=4,'tensor'=4] {'tensor'}, dimensions={0}, use_global_device_ids=true | all-gather | bytes 327680 | tf_op jit(solution)/shard_map/all_gather | solution.py:333
  229.2 1.1 fusion
  230.3 5.9 %all_gather.11 = bf16[1024,128]{1,0:T(8,128)(2,1)S(1)} all-gather(bf16[256,128]{1,0:T(8,128)(2,1)S(1)} %get-tuple-element.18), channel_id=1, replica_groups=mesh['pipe'=2,'expert'=4,'tensor'=4] {'tensor'}, dimensions={0}, use_global_device_ids=true | all-gather | bytes 327680 | tf_op jit(solution)/shard_map/all_gather | solution.py:334
  236.1 1.5 fusion.1
  237.7 0.0 copy-start.1
  237.7 1.7 fusion.18
  239.4 0.9 copy.41
  (13 shorter events, 0.1 us)
Async XLA Ops:
  7.2 1.2 copy-start
  7.2 163.4 %all-gather.2.cloned.1.call-start = ((), (), s32[]{:S(2)}) async-start(), calls=%async_computation.1 | async-start | bytes 3538944 | tf_op jit(solution)/shard_map/all_gather | solution.py:320
  99.4 3.5 %copy-start.5 = (s32[128,2]{0,1:T(2,128)S(1)}, s32[128,2]{0,1:T(2,128)}, u32[]{:S(2)}) copy-start(s32[128,2]{0,1:T(2,128)} %param.16) | copy-start | bytes 3076
  99.4 3.6 %copy-start.2 = (bf16[128,1536]{1,0:T(8,128)(2,1)S(1)}, bf16[128,1536]{1,0:T(8,128)(2,1)}, u32[]{:S(2)}) copy-start(bf16[128,1536]{1,0:T(8,128)(2,1)} %param.12) | copy-start | bytes 1179652
  99.4 10.0 %copy-start.4 = (f32[1536]{0:T(1024)S(1)}, f32[1536]{0:T(1024)}, u32[]{:S(2)}) copy-start(f32[1536]{0:T(1024)} %param.14) | copy-start | bytes 18436
  103.3 75.2 %copy-start.3 = (bf16[128,1536]{1,0:T(8,128)(2,1)}, bf16[128,1536]{1,0:T(8,128)(2,1)S(1)}, u32[]{:S(2)}) copy-start(bf16[128,1536]{1,0:T(8,128)(2,1)S(1)} %get-tuple-element.11) | copy-start | bytes 1179652
  110.4 111.4 %reduce-scatter.2.cloned.1.call-start = ((), (), s32[]{:S(2)}) async-start(), calls=%async_computation.2 | async-start | bytes 5242880 | tf_op jit(solution)/shard_map/reduce_scatter | solution.py:324
  237.7 2.6 %copy-start.1 = (f32[1536,4]{0,1:T(4,128)S(1)}, f32[1536,4]{0,1:T(4,128)}, u32[]{:S(2)}) copy-start(f32[1536,4]{0,1:T(4,128)} %param.15) | copy-start | bytes 73732
Sparse Core Ops, SparseCore 0:
  110.5 59.9 all-gather.1
  178.7 43.1 reduce-scatter.1

commit v2 on v1

--- a/solution.py
+++ b/solution.py
@@ -258,6 +258,275 @@
     )(going, gate, up, down)
 
 
+def attend_kernel(
+    np_, ne, nt, x_in, gain, wq_hbm, wk_hbm, wv_hbm, out,
+    xs, w, lhs, sq, mine, theirs, q, kv,
+    w_sem, own_sem, zs, zr, ys, yr, ps, pr, ks, kr,
+):
+    p = lax.axis_index("pipe")
+    e = lax.axis_index("expert")
+    t = lax.axis_index("tensor")
+    tb, width = x_in.shape
+    qw = wq_hbm.shape[1]
+    cols = w.shape[1] + HD
+    groups = np_ * ne
+    qr = groups * tb // nt
+    per = qr // tb
+    heads = qw // HD
+    head = (p * ne + e) * heads // (QH // KVH)
+    at_head = pl.ds(pl.multiple_of(head * HD, 128), HD)
+    loads = [
+        pltpu.make_async_copy(wq_hbm, w.at[:, pl.ds(0, qw)], w_sem.at[0]),
+        pltpu.make_async_copy(wk_hbm.at[:, at_head], w.at[:, pl.ds(qw, HD)], w_sem.at[1]),
+        pltpu.make_async_copy(wv_hbm.at[:, at_head], w.at[:, pl.ds(qw + HD, HD)], w_sem.at[2]),
+    ]
+    for load in loads:
+        load.start()
+    own = pltpu.make_async_copy(x_in, xs.at[0, e], own_sem)
+    own.start()
+
+    barrier = pltpu.get_barrier_semaphore()
+    peers = [(p, lax.rem(e + de, ne), t) for de in range(1, ne)]
+    peers += [(lax.rem(p + dp, np_), e, t) for dp in range(1, np_)]
+    peers += [(p, e, lax.rem(t + dt, nt)) for dt in range(1, nt)]
+    for peer in peers:
+        pl.semaphore_signal(barrier, inc=1, device_id=peer, device_id_type=MESH)
+    pl.semaphore_wait(barrier, len(peers))
+    own.wait()
+
+    def copy(src, dst, s_sem, r_sem, peer):
+        return pltpu.make_async_remote_copy(
+            src_ref=src, dst_ref=dst, send_sem=s_sem, recv_sem=r_sem,
+            device_id=peer, device_id_type=MESH,
+        )
+
+    def shift(d, s):
+        return lax.rem(e + (ne - s if d == 0 else s), ne)
+
+    def valid(d, s):
+        return e >= s if d == 0 else e + s < ne
+
+    def onward(d, s):
+        block = xs.at[0, shift(d, s - 1)]
+        return copy(block, block, zs.at[d, s], zr.at[d, s], (p, shift(1 - d, 1), t))
+
+    def may_send(d, s):
+        ahead = e + 1 < ne if d == 0 else e >= 1
+        return jnp.logical_and(ahead, valid(d, s - 1))
+
+    def across(dp, d, s):
+        return copy(
+            xs.at[0, shift(d, s)], xs.at[np_ - dp, shift(d, s)],
+            ys.at[dp, d, s], yr.at[np_ - dp, d, s], (lax.rem(p + dp, np_), e, t),
+        )
+
+    def number(dp, row):
+        return lax.rem(p + dp, np_) * ne + row
+
+    def hand_over(dp, row):
+        b = number(dp, row)
+        return copy(
+            mine.at[dp, row], theirs.at[t, lax.rem(b, per)],
+            ps.at[dp, row], pr.at[t, lax.rem(b, per)], (p, e, b // per),
+        )
+
+    lt = lane_tile(width)
+    ct = lane_tile(cols - HD)
+
+    def project(dp, row):
+        sq[...] = jnp.zeros_like(sq)
+
+        def scale(n, carry):
+            at = pl.ds(pl.multiple_of(n * lt, lt), lt)
+            value = xs[dp, row, :, at].astype(jnp.float32)
+            scaled = value * gain[:, at]
+            lhs[:, at] = jnp.clip(scaled, -1e30, 1e30).astype(jnp.bfloat16)
+            square = value * value
+            for i in range(lt // 128):
+                sq[...] += square[:, i * 128 : (i + 1) * 128]
+            return carry
+
+        lax.fori_loop(0, width // lt, scale, 0)
+
+        def tile(n, carry):
+            at = pl.ds(pl.multiple_of(n * ct, ct), ct)
+            y = jnp.dot(lhs[...], w[:, at], preferred_element_type=jnp.float32)
+            mine[dp, row, :, at] = y.astype(jnp.bfloat16)
+            return carry
+
+        lax.fori_loop(0, (cols - HD) // ct, tile, 0)
+        total = jnp.sum(sq[...], axis=1, keepdims=True)
+        high = total.astype(jnp.bfloat16).astype(jnp.float32)
+        rest = jnp.where(high < 3e38, total - high, 0.0)
+        middle = rest.astype(jnp.bfloat16).astype(jnp.float32)
+        lane = lax.broadcasted_iota(jnp.int32, (tb, HD), 1)
+        packed = jnp.where(lane == 0, high, 0.0)
+        packed = jnp.where(lane == 1, middle, packed)
+        packed = jnp.where(lane == 2, rest - middle, packed)
+        mine[dp, row, :, pl.ds(cols - HD, HD)] = packed.astype(jnp.bfloat16)
+
+        @pl.when(number(dp, row) // per != t)
+        def _():
+            hand_over(dp, row).start()
+
+    def start_from(d, s):
+        if s + 1 < ne:
+            @pl.when(may_send(d, s + 1))
+            def _():
+                onward(d, s + 1).start()
+
+    def start_across(d, s):
+        for dp in range(1, np_):
+            across(dp, d, s).start()
+
+    def take_across(d, s):
+        for dp in range(1, np_):
+            across(np_ - dp, d, s).wait_recv()
+            project(dp, shift(d, s))
+
+    start_from(0, 0)
+    start_from(1, 0)
+    start_across(0, 0)
+    for load in loads:
+        load.wait()
+    project(0, shift(0, 0))
+    steps = [(0, 0)]
+    for s in range(1, ne):
+        for d in range(2):
+            @pl.when(valid(d, s))
+            def _(d=d, s=s):
+                arrived = xs.at[0, shift(d, s)]
+                copy(arrived, arrived, zs.at[d, s], zr.at[d, s], (p, e, t)).wait_recv()
+                start_from(d, s)
+                start_across(d, s)
+        for d in range(2):
+            @pl.when(valid(d, s))
+            def _(d=d, s=s):
+                project(0, shift(d, s))
+        if s == 1:
+            take_across(0, 0)
+        else:
+            for d in range(2):
+                @pl.when(valid(d, s - 1))
+                def _(d=d, s=s):
+                    take_across(d, s - 1)
+    for d in range(2):
+        @pl.when(valid(d, ne - 1))
+        def _(d=d):
+            take_across(d, ne - 1)
+
+    for i in range(per):
+        b = t * per + i
+        own_dp = lax.rem(b // ne + np_ - p, np_)
+        total = mine[own_dp, lax.rem(b, ne)].astype(jnp.float32)
+        for dt in range(1, nt):
+            other = lax.rem(t + dt, nt)
+            block = theirs.at[other, i]
+            copy(block, block, ps.at[0, 0], pr.at[other, i], (p, e, other)).wait_recv()
+            total = total + theirs[other, i].astype(jnp.float32)
+        squares = jnp.sum(total[:, cols - HD :], axis=1, keepdims=True)
+        value = total[:, : cols - HD] * lax.rsqrt(squares / D + NORM_EPS)
+        value = value.astype(jnp.bfloat16)
+        q[i * tb : (i + 1) * tb, :] = value[:, :qw]
+        kv[t, i * tb : (i + 1) * tb, :] = value[:, qw:]
+
+    shares = [
+        copy(kv.at[t], kv.at[t], ks.at[dt], kr.at[nt - dt], (p, e, lax.rem(t + dt, nt)))
+        for dt in range(1, nt)
+    ]
+    for share in shares:
+        share.start()
+    for dt in range(1, nt):
+        block = kv.at[lax.rem(t + dt, nt)]
+        copy(block, block, ks.at[dt], kr.at[dt], (p, e, lax.rem(t + dt, nt))).wait_recv()
+
+    tokens = nt * qr
+
+    def one_head(h, carry):
+        at = pl.ds(pl.multiple_of(h * HD, HD), HD)
+        keys = kv[:, :, 0:HD].reshape(tokens, HD)
+        values = kv[:, :, HD : 2 * HD].reshape(tokens, HD)
+        scores = lax.dot_general(
+            q[:, at], keys, (((1,), (1,)), ((), ())), preferred_element_type=jnp.float32
+        ) * (1.0 / math.sqrt(HD))
+        row = t * qr + lax.broadcasted_iota(jnp.int32, scores.shape, 0)
+        allowed = lax.broadcasted_iota(jnp.int32, scores.shape, 1) <= row
+        scores = jnp.where(allowed, scores, -1e30)
+        best = jnp.max(scores, axis=1, keepdims=True)
+        weights = jnp.where(allowed, jnp.exp(scores - best), 0.0)
+        total = jnp.sum(weights, axis=1, keepdims=True)
+        context = jnp.dot(
+            weights.astype(jnp.bfloat16), values, preferred_element_type=jnp.float32
+        )
+        out[:, at] = (context / total).astype(jnp.bfloat16)
+        return carry
+
+    lax.fori_loop(0, heads, one_head, 0)
+
+    for share in shares:
+        share.wait_send()
+    for s in range(ne):
+        for d in range(2):
+            if s:
+                @pl.when(may_send(d, s))
+                def _(d=d, s=s):
+                    onward(d, s).wait_send()
+            if s or d == 0:
+                @pl.when(valid(d, s))
+                def _(d=d, s=s):
+                    for dp in range(1, np_):
+                        across(dp, d, s).wait_send()
+    for dp in range(np_):
+        for row in range(ne):
+            @pl.when(number(dp, row) // per != t)
+            def _(dp=dp, row=row):
+                hand_over(dp, row).wait_send()
+
+
+def attention_layer(x, gain, wq, wk, wv, sizes):
+    np_, ne, nt = sizes
+    tb, width = x.shape
+    qw = wq.shape[1]
+    cols = qw + 3 * HD
+    qr = np_ * ne * tb // nt
+    per = qr // tb
+    dma = pltpu.SemaphoreType.DMA
+    bf, f32 = jnp.bfloat16, jnp.float32
+    vm = pl.BlockSpec(memory_space=pltpu.VMEM)
+    hbm = pl.BlockSpec(memory_space=pl.ANY)
+    return pl.pallas_call(
+        functools.partial(attend_kernel, np_, ne, nt),
+        out_shape=jax.ShapeDtypeStruct((qr, qw), bf),
+        in_specs=[vm, vm, hbm, hbm, hbm],
+        out_specs=vm,
+        scratch_shapes=[
+            pltpu.VMEM((np_, ne, tb, width), bf),
+            pltpu.VMEM((width, qw + 2 * HD), bf),
+            pltpu.VMEM((tb, width), bf),
+            pltpu.VMEM((tb, HD), f32),
+            pltpu.VMEM((np_, ne, tb, cols), bf),
+            pltpu.VMEM((nt, per, tb, cols), bf),
+            pltpu.VMEM((qr, qw), bf),
+            pltpu.VMEM((nt, qr, 2 * HD), bf),
+            dma((3,)),
+            dma,
+            dma((2, ne)), dma((2, ne)),
+            dma((np_, 2, ne)), dma((np_, 2, ne)),
+            dma((np_, ne)), dma((nt, per)),
+            dma((nt,)), dma((nt,)),
+        ],
+        compiler_params=pltpu.CompilerParams(
+            collective_id=1, has_side_effects=True, vmem_limit_bytes=48 * MIB
+        ),
+        cost_estimate=pl.CostEstimate(
+            flops=2 * np_ * ne * tb * width * cols,
+            bytes_accessed=2 * width * cols,
+            transcendentals=0,
+        ),
+        name="attention_layer",
+    )(x, gain.reshape(1, width), wq, wk, wv)
+
+
 def on_device(
     stream,
     norm_gain,
@@ -304,51 +573,7 @@
     picked_rows = padded[target].astype(jnp.float32)
     moe_sum = mixing[:, 0:1] * picked_rows[:, 0] + mixing[:, 1:2] * picked_rows[:, 1]
     new_stream = (stream_f + moe_sum).astype(jnp.bfloat16)
-    attn_f = new_stream.astype(jnp.float32)
-    square_two = lax.psum(jnp.sum(attn_f * attn_f, axis=1), "tensor")
-    attn_in = (attn_f * lax.rsqrt(square_two / D + NORM_EPS)[:, None] * attn_gain).astype(
-        jnp.bfloat16
-    )
-    head_group = lax.axis_index(("pipe", "expert"))
-    query_width = w_query.shape[1]
-    heads_here = query_width // HD
-    shared_head = head_group * heads_here // (QH // KVH)
-    key_columns = lax.dynamic_slice_in_dim(w_key, shared_head * HD, HD, 1)
-    value_columns = lax.dynamic_slice_in_dim(w_value, shared_head * HD, HD, 1)
-    projector = jnp.concatenate([w_query, key_columns, value_columns], axis=1)
-    partial_proj = jnp.dot(
-        lax.all_gather(attn_in, ("pipe", "expert"), axis=0, tiled=True),
-        projector,
-        preferred_element_type=jnp.float32,
-    )
-    own_proj = lax.psum_scatter(partial_proj, "tensor", scatter_dimension=0, tiled=True)
-    query_rows = own_proj.shape[0]
-    queries = own_proj[:, :query_width].astype(jnp.bfloat16).reshape(query_rows, heads_here, HD)
-    key_rows = own_proj[:, query_width : query_width + HD].astype(jnp.bfloat16)
-    value_rows = own_proj[:, query_width + HD :].astype(jnp.bfloat16)
-    first_row = lax.axis_index("tensor") * query_rows
-    query_pos = first_row + jnp.arange(query_rows, dtype=jnp.int32)
-    score_scale = 1.0 / math.sqrt(HD)
-    best = jnp.full((heads_here, query_rows), -1e30, jnp.float32)
-    key_piece = lax.all_gather(key_rows, "tensor", axis=0, tiled=True)
-    value_piece = lax.all_gather(value_rows, "tensor", axis=0, tiled=True)
-    key_pos = jnp.arange(key_piece.shape[0], dtype=jnp.int32)
-    allowed = (key_pos[None, :] <= query_pos[:, None])[None, :, :]
-    scores = (
-        jnp.einsum("qhd,kd->hqk", queries, key_piece, preferred_element_type=jnp.float32)
-        * score_scale
-    )
-    scores = jnp.where(allowed, scores, -1e30)
-    new_best = jnp.maximum(best, jnp.max(scores, axis=2))
-    weights = jnp.where(allowed, jnp.exp(scores - new_best[:, :, None]), 0.0)
-    total = jnp.sum(weights, axis=2)
-    update = jnp.einsum(
-        "hqk,kd->hqd", weights.astype(jnp.bfloat16), value_piece, preferred_element_type=jnp.float32
-    )
-    accum = update
-    best, total, accum = (new_best, total, accum)
-    context = accum / total[:, :, None]
-    attended = context.transpose(1, 0, 2).reshape(query_rows, query_width).astype(jnp.bfloat16)
+    attended = attention_layer(new_stream, attn_gain, w_query, w_key, w_value, sizes)
     return (new_stream, attended)
 
 

time: 248 us -> 160 us (0.65)
  waiting for transfers between devices: 102 us -> 0 us
  Pallas kernels: 74.1 us -> 136 us
  blocking collectives: 26.1 us -> 8.34 us
  between operations: 14.3 us -> 0.85 us
  matrix products: 12.5 us -> 1.71 us
  other arithmetic: 7.27 us -> 2.56 us
    pallas_call x0 -> x1, Pallas kernels: none -> 61.5 us  [attention_layer(): pl.pallas_call(functools.partial(attend_kernel, np_, ne, nt), out_shape=j...]
    all_gather x1 -> x0, waiting for transfers between devices: 58.7 us -> none  [on_device(): lax.all_gather(attn_in, ('pipe', 'expert'), axis=0, tiled=True)]
    reduce_scatter x1 -> x0, waiting for transfers between devices: 43.1 us -> none  [on_device(): lax.psum_scatter(partial_proj, 'tensor', scatter_dimension=0, tiled=True)]
    all_gather x2 -> x0, blocking collectives: 11.7 us -> none  [the longest x1 5.87 us: on_device(): value_piece = lax.all_gather(value_rows, 'tensor', axis=0, tiled=True)]
    dot_general x3 -> x0, matrix products: 10.7 us -> none  [the longest x1 7.95 us: on_device(): jnp.dot(lax.all_gather(attn_in, ('pipe', 'expert'), axis=0, tiled=True),...]
    psum x1 -> x0, blocking collectives: 6.14 us -> none  [on_device(): square_two = lax.psum(jnp.sum(attn_f * attn_f, axis=1), 'tensor')]
  transfers between devices with their start and end apart: 2 -> 0, of which waited for: 2 -> 0; matrix products, arithmetic and copies ran while one was open for 1% -> 0% of each run, Pallas kernels for 0% -> 0%
where the time goes in v2:
time: 160 us; the launch traced here: 159 us
  Pallas kernels  136 us (85%)
  local copies, waits for them, and re-layouts  10 us (6%)
  blocking collectives  8.34 us (5%)
  other arithmetic  2.56 us (2%)
  matrix products  1.71 us (1%)
    pallas_call x1, Pallas kernels, expert_layer(): pl.pallas_call(functools.partial(expert_kernel, np_, ne, nt, going.shape)...  74.1 us
    pallas_call x1, Pallas kernels, attention_layer(): pl.pallas_call(functools.partial(attend_kernel, np_, ne, nt), out_shape=j...  61.5 us
    psum x1, blocking collectives, on_device(): squares, logit_sum = lax.psum((square_part, logit_part), 'tensor')  8.34 us

profile of v2, /device:TPU:0, one launch (start us, length us, event | category | flops | bytes accessed | tf_op | source)
XLA Modules:
  0.0 159.1 jit_solution(994068101610642335)
XLA Ops:
  0.6 0.0 copy-start
  0.6 0.0 copy-start.5
  0.7 0.0 copy-start.6
  0.7 0.7 copy-done
  1.4 1.7 %fusion.1 = f32[128,4]{0,1:T(4,128)S(1)} fusion(f32[1536,4]{0,1:T(4,128)S(1)} %copy-done, bf16[128,1536]{1,0:T(8,128)(2,1)} %param.12, f32[1536]{0:T(1024)} %param.13), kind=kOutput, calls=%fused_computation.6 | convolution fusion | flops 9830400 | bytes 425984 | tf_op jit(solution)/shard_map/dot_general | solution.py:549
  3.1 1.2 fusion.3
  4.3 8.3 %all-reduce.1 = (f32[128]{0:T(128)S(1)}, f32[128,4]{0,1:T(4,128)S(1)}) all-reduce(f32[128]{0:T(128)S(1)} %fusion.3, f32[128,4]{0,1:T(4,128)S(1)} %fusion.1), channel_id=1, replica_groups=mesh['pipe'=2,'expert'=4,'tensor'=4] {'tensor'}, use_global_device_ids=true, to_apply=%region_1.0 | all-reduce | flops 640 | bytes 5120 | tf_op jit(solution)/shard_map/psum | solution.py:550
  12.6 1.1 fusion.2
  13.7 0.4 broadcast_in_dim.40
  14.1 0.3 reshape.69
  14.4 0.0 copy-done.5
  14.5 0.0 copy-done.6
  14.5 0.1 copy.22
  14.6 0.1 reshape.52
  14.7 1.9 %scatter_custom_fusion = bf16[161,1536]{1,0:T(8,128)(2,1)S(1)} fusion(s32[256]{0:T(256)S(1)} %bitcast.27, bf16[256,1536]{1,0:T(8,128)(2,1)S(1)} %reshape.69, bf16[]{:T(256)} %constant.2.clone.1), kind=kCustom, calls=%fused_computation.16 | custom fusion | bytes 494594 | tf_op jit(solution)/shard_map/scatter | solution.py:566
  16.6 0.8 slice.22
  17.5 74.1 %expert_layer.1 = bf16[4,40,1536]{2,1,0:T(8,128)(2,1)} custom-call(bf16[4,40,1536]{2,1,0:T(8,128)(2,1)} %bitcast.25, bf16[6144,1024]{1,0:T(8,128)(2,1)} %bitcast.28, bf16[6144,1024]{1,0:T(8,128)(2,1)} %bitcast.29, bf16[1024,6144]{1,0:T(8,128)(2,1)} %bitcast.30), custom_call_target="tpu_custom_call" | custom-call | flops 12079595520 | bytes 37748736 | tf_op jit(solution)/shard_map/expert_layer/pallas_call | solution.py:222
  91.6 1.1 concatenate.3
  92.6 0.1 copy.23
  92.7 0.1 reshape.59
  92.9 1.3 gather_fusion
  94.2 0.0 copy-start.3
  94.2 1.0 reshape.75
  95.1 0.0 copy-start.4
  95.2 0.0 copy-start.2
  95.2 1.2 fusion.11
  96.4 0.0 copy-done.3
  96.4 0.2 fusion.4.x_in
  96.7 0.0 copy-done.4
  96.7 0.0 copy-start.1
  96.7 0.1 copy-done.2
  96.8 61.5 %attention_layer.1 = bf16[256,768]{1,0:T(8,128)(2,1)S(1)} custom-call(bf16[128,1536]{1,0:T(8,128)(2,1)S(1)} %fusion.4.x_in, f32[1,1536]{1,0:T(1,128)S(1)} %reshape.56.gain, bf16[1536,768]{1,0:T(8,128)(2,1)S(1)} %copy-done.2, bf16[1536,1024]{1,0:T(8,128)(2,1)} %wk_hbm.1, bf16[1536,1024]{1,0:T(8,128)(2,1)} %wv_hbm.1), custom_call_target="tpu_custom_call" | custom-call | flops 3623878656 | bytes 3538944 | tf_op jit(solution)/shard_map/attention_layer/pallas_call | solution.py:497
  158.4 0.0 copy-done.1
  158.4 0.7 copy.41
  (8 shorter events, 0.1 us)
Async XLA Ops:
  0.6 0.7 copy-start
  0.6 13.8 %copy-start.5 = (s32[128,2]{0,1:T(2,128)S(1)}, s32[128,2]{0,1:T(2,128)}, u32[]{:S(2)}) copy-start(s32[128,2]{0,1:T(2,128)} %param.16) | copy-start | bytes 3076
  0.7 13.8 %copy-start.6 = (s32[128,2]{0,1:T(2,128)S(1)}, s32[128,2]{0,1:T(2,128)}, u32[]{:S(2)}) copy-start(s32[128,2]{0,1:T(2,128)} %param.17) | copy-start | bytes 3076
  94.2 2.3 %copy-start.3 = (bf16[128,1536]{1,0:T(8,128)(2,1)S(1)}, bf16[128,1536]{1,0:T(8,128)(2,1)}, u32[]{:S(2)}) copy-start(bf16[128,1536]{1,0:T(8,128)(2,1)} %param.12) | copy-start | bytes 1179652
  95.1 1.5 copy-start.4
  95.2 1.7 %copy-start.2 = (bf16[1536,768]{1,0:T(8,128)(2,1)S(1)}, bf16[1536,768]{1,0:T(8,128)(2,1)}, u32[]{:S(2)}) copy-start(bf16[1536,768]{1,0:T(8,128)(2,1)} %wq_hbm.1) | copy-start | bytes 7077892
  96.7 61.7 %copy-start.1 = (bf16[128,1536]{1,0:T(8,128)(2,1)}, bf16[128,1536]{1,0:T(8,128)(2,1)S(1)}, u32[]{:S(2)}) copy-start(bf16[128,1536]{1,0:T(8,128)(2,1)S(1)} %fusion.4.x_in) | copy-start | bytes 1179652

commit v3 on v2

--- a/solution.py
+++ b/solution.py
@@ -44,6 +44,7 @@
         return (p, lax.rem(e + de, ne), t)
 
     chips = [(dc, dp) for dc in range(nc) for dp in range(np_) if (dc, dp) != (0, 0)]
+    straight = [(dc, dp) for dc, dp in chips if dc == 0 or dp == 0]
     order = [(dc, dk) for dc in range(nc) for dk in range(2)]
 
     own = pltpu.make_async_copy(going.at[e], rows.at[0, 0, 0, 0], own_sem)
@@ -101,7 +102,7 @@
     for de in zorder:
         if de:
             landed(rows.at[0, 0, 0, de], zs.at[de], zr.at[de])
-        for dc, dp in chips:
+        for dc, dp in straight:
             oc, op = (nc - dc) % nc, (np_ - dp) % np_
             sent.append(send(
                 rows.at[0, 0, 0, de], rows.at[oc, 0, op, de],
@@ -109,12 +110,25 @@
             ))
         to_sibling(0, 0, de)
 
-    def arrivals(dc):
-        for de in zorder:
-            for dp in range(np_):
-                if (dc, dp) != (0, 0):
-                    landed(rows.at[dc, 0, dp, de], cs.at[dc, dp, de], cr.at[dc, dp, de])
-                    to_sibling(dc, dp, de)
+    def came(dc, dp, de):
+        landed(rows.at[dc, 0, dp, de], cs.at[dc, dp, de], cr.at[dc, dp, de])
+        to_sibling(dc, dp, de)
+
+    for de in zorder:
+        for dc, dp in straight:
+            came(dc, dp, de)
+            if dc == 0 and de % 2:
+                for far in range(1, nc):
+                    sent.append(send(
+                        rows.at[0, 0, dp, de], rows.at[nc - far, 0, dp, de],
+                        cs.at[far, dp, de], cr.at[nc - far, dp, de], chip(far, 0),
+                    ))
+            if dp == 0 and de % 2 == 0:
+                for far in range(1, np_):
+                    sent.append(send(
+                        rows.at[dc, 0, 0, de], rows.at[dc, 0, np_ - far, de],
+                        cs.at[dc, far, de], cr.at[dc, np_ - far, de], chip(0, far),
+                    ))
 
     lt = lane_tile(width)
     ht = lane_tile(hidden)
@@ -152,10 +166,14 @@
         lax.fori_loop(0, hidden // ht, tile, 0)
 
     for dc in range(nc):
-        arrivals(dc)
+        if dc:
+            for de in zorder:
+                for dp in range(1, np_):
+                    came(dc, dp, de)
         for dk in range(2):
             gate_up(dc * 2 + dk, dc, dk)
 
+    zlast = list(range(1, ne)) + [0]
     for dc in reversed(range(nc)):
         j = dc * 2 + 1
         loads["d", j].wait()
@@ -179,23 +197,52 @@
 
         lax.fori_loop(0, width // lt, own_tile, 0)
         landed(sib_in.at[dc], bs.at[dc], br.at[dc])
-        for de in list(range(1, ne)) + [0]:
-            for dp in range(np_):
-                if (dc, dp) != (0, 0):
-                    tgt_out[dc, dp, de] = (
-                        part[dp, de] + sib_in[dc, dp, de].astype(jnp.float32)
-                    ).astype(jnp.bfloat16)
-                    oc, op = (nc - dc) % nc, (np_ - dp) % np_
-                    sent.append(send(
-                        tgt_out.at[dc, dp, de], tgt_in.at[oc, op, de],
-                        ts.at[dc, dp, de], tr.at[oc, op, de], chip(dc, dp),
-                    ))
-
-    for de in list(range(1, ne)) + [0]:
+
+        def partial(dp, de, dc=dc):
+            return part[dp, de] + sib_in[dc, dp, de].astype(jnp.float32)
+
+        def ship(dc, dp, de, slot, peer):
+            sent.append(send(
+                tgt_out.at[dc, dp, de], tgt_in.at[slot], ts.at[dc, dp, de], tr.at[slot], peer
+            ))
+
+        def collect(dc, dp, de):
+            landed(tgt_in.at[dc, dp, de], ts.at[dc, dp, de], tr.at[dc, dp, de])
+            return tgt_in[dc, dp, de].astype(jnp.float32)
+
+        if dc:
+            for de in zlast:
+                for dp in range(1, np_):
+                    tgt_out[dc, dp, de] = partial(dp, de).astype(jnp.bfloat16)
+                    if de % 2:
+                        ship(dc, dp, de, (dc, np_ - dp, de), chip(0, dp))
+                    else:
+                        ship(dc, dp, de, (nc - dc, dp, de), chip(dc, 0))
+            for de in zlast:
+                tgt_out[dc, 0, de] = partial(0, de).astype(jnp.bfloat16)
+                if de % 2 == 0:
+                    ship(dc, 0, de, (nc - dc, 0, de), chip(dc, 0))
+        else:
+            for de in zlast:
+                if de % 2:
+                    for far in range(1, nc):
+                        total = tgt_out[far, 0, de].astype(jnp.float32)
+                        for dp in range(1, np_):
+                            total = total + collect(far, dp, de)
+                        tgt_out[far, 0, de] = total.astype(jnp.bfloat16)
+                        ship(far, 0, de, (nc - far, 0, de), chip(far, 0))
+                for dp in range(1, np_):
+                    total = partial(dp, de)
+                    if de % 2 == 0:
+                        for far in range(1, nc):
+                            total = total + collect(far, dp, de)
+                    tgt_out[0, dp, de] = total.astype(jnp.bfloat16)
+                    ship(0, dp, de, (0, np_ - dp, de), chip(0, dp))
+
+    for de in zlast:
         total = part[0, de] + sib_in[0, 0, de].astype(jnp.float32)
-        for dc, dp in chips:
-            landed(tgt_in.at[dc, dp, de], ts.at[dc, dp, de], tr.at[dc, dp, de])
-            total = total + tgt_in[dc, dp, de].astype(jnp.float32)
+        for dc, dp in straight:
+            total = total + collect(dc, dp, de)
         if de:
             zbuf[de] = total.astype(jnp.bfloat16)
             sent.append(send(
@@ -557,21 +604,19 @@
     mixing = jnp.stack([first_share, 1.0 - first_share], axis=1)
     slot_total = experts * CAP
     target = jnp.where(expert_slots >= 0, expert_ids * CAP + expert_slots, slot_total)
-    copies = jnp.broadcast_to(normed[:, None, :], (token_rows, 2, local_width)).reshape(
-        token_rows * 2, local_width
+    slots = jnp.arange(slot_total, dtype=jnp.int32).reshape(experts, CAP, 1)
+    place = ((target[:, 0] == slots) | (target[:, 1] == slots)).astype(jnp.bfloat16)
+    outgoing = jnp.einsum(
+        "eci,id->ecd", place, normed, preferred_element_type=jnp.float32
+    ).astype(jnp.bfloat16)
+    sizes = tuple(lax.axis_size(name) for name in ("pipe", "expert", "tensor"))
+    returned = expert_layer(outgoing, w_gate[0], w_up[0], w_down[0], sizes)
+    columns = slots.reshape(1, experts, CAP)
+    combine = jnp.where(target[:, 0, None, None] == columns, mixing[:, 0, None, None], 0.0)
+    combine += jnp.where(target[:, 1, None, None] == columns, mixing[:, 1, None, None], 0.0)
+    moe_sum = jnp.einsum(
+        "iec,ecd->id", combine, returned.astype(jnp.float32), precision=lax.Precision.HIGHEST
     )
-    outgoing = (
-        jnp.zeros((slot_total + 1, local_width), jnp.bfloat16)
-        .at[target.reshape(-1)]
-        .set(copies)[:slot_total]
-    )
-    sizes = tuple(lax.axis_size(name) for name in ("pipe", "expert", "tensor"))
-    returned = expert_layer(
-        outgoing.reshape(experts, CAP, local_width), w_gate[0], w_up[0], w_down[0], sizes
-    ).reshape(slot_total, local_width)
-    padded = jnp.concatenate([returned, jnp.zeros((1, local_width), jnp.bfloat16)], axis=0)
-    picked_rows = padded[target].astype(jnp.float32)
-    moe_sum = mixing[:, 0:1] * picked_rows[:, 0] + mixing[:, 1:2] * picked_rows[:, 1]
     new_stream = (stream_f + moe_sum).astype(jnp.bfloat16)
     attended = attention_layer(new_stream, attn_gain, w_query, w_key, w_value, sizes)
     return (new_stream, attended)

time: 160 us -> 153 us (0.956)
  local copies, waits for them, and re-layouts: 10 us -> 3.14 us
  Pallas kernels: 136 us -> 131 us
  matrix products: 1.71 us -> 5.49 us
    pallas_call x1, Pallas kernels: 74.1 us -> 68.5 us  [expert_layer(): pl.pallas_call(functools.partial(expert_kernel, np_, ne, nt, going.shape)...]
    dot_general x0 -> x2, matrix products: none -> 3.77 us  [the longest x1 2.12 us: on_device(): jnp.einsum('eci,id->ecd', place, normed, preferred_element_type=jnp.float32)]
    slice x2 -> x0, local copies, waits for them, and re-layouts: 2.03 us -> none  [the longest x1 1.21 us: on_device(): picked_rows[:, 0]]
    scatter x1 -> x0, local copies, waits for them, and re-layouts: 1.89 us -> none  [on_device(): outgoing = jnp.zeros((slot_total + 1, local_width), jnp.bfloat16).at[targ...]
where the time goes in v3:
time: 153 us; the launch traced here: 152 us
  Pallas kernels  131 us (86%)
  blocking collectives  8.33 us (5%)
  matrix products  5.49 us (4%)
  local copies, waits for them, and re-layouts  3.14 us (2%)
  other arithmetic  2.6 us (2%)
    pallas_call x1, Pallas kernels, expert_layer(): pl.pallas_call(functools.partial(expert_kernel, np_, ne, nt, going.shape)...  68.5 us
    pallas_call x1, Pallas kernels, attention_layer(): pl.pallas_call(functools.partial(attend_kernel, np_, ne, nt), out_shape=j...  62.8 us
    psum x1, blocking collectives, on_device(): squares, logit_sum = lax.psum((square_part, logit_part), 'tensor')  8.33 us

profile of v3, /device:TPU:0, one launch (start us, length us, event | category | flops | bytes accessed | tf_op | source)
XLA Modules:
  0.0 151.6 jit_solution(14908015385626417913)
XLA Ops:
  0.6 0.0 copy-start
  0.6 1.2 fusion.5
  1.8 0.7 compare_select_fusion
  2.5 0.0 copy-done
  2.5 1.7 %fusion.3 = f32[128,4]{0,1:T(4,128)S(1)} fusion(f32[1536,4]{0,1:T(4,128)S(1)} %copy-done, bf16[128,1536]{1,0:T(8,128)(2,1)} %param.12, f32[1536]{0:T(1024)} %param.13), kind=kOutput, calls=%fused_computation.7 | convolution fusion | flops 9830400 | bytes 425984 | tf_op jit(solution)/shard_map/dot_general | solution.py:596
  4.2 8.3 %all-reduce = (f32[128]{0:T(128)S(1)}, f32[128,4]{0,1:T(4,128)S(1)}) all-reduce(f32[128]{0:T(128)S(1)} %fusion.5, f32[128,4]{0,1:T(4,128)S(1)} %fusion.3), channel_id=1, replica_groups=mesh['pipe'=2,'expert'=4,'tensor'=4] {'tensor'}, use_global_device_ids=true, to_apply=%region_1.0 | all-reduce | flops 640 | bytes 5120 | tf_op jit(solution)/shard_map/psum | solution.py:597
  12.6 0.7 select_reduce_fusion
  13.3 0.7 reshape.61.gain
  14.0 2.1 %convolution_convert_fusion.going = bf16[4,40,1536]{2,1,0:T(8,128)(2,1)} fusion(bf16[128,1536]{1,0:T(8,128)(2,1)} %param.12, f32[128]{0:T(128)S(1)} %add_rsqrt_fusion, f32[1536]{0:T(1024)} %param.13, s32[128]{0:T(128)S(1)} %get-tuple-element.7, s32[4,40]{1,0:T(4,128)S(1)} %multiply_add_fusion, s32[128]{0:T(128)S(1)} %get-tuple-element.6), kind=kOutput, calls=%fused_computation.2 | convolution fusion | flops 64008192 | bytes 893056 | tf_op jit(solution)/shard_map/eci,id->ecd/dot_general | solution.py:609
  16.1 0.0 copy-start.3
  16.1 68.5 %expert_layer.1 = bf16[4,40,1536]{2,1,0:T(8,128)(2,1)} custom-call(bf16[4,40,1536]{2,1,0:T(8,128)(2,1)} %convolution_convert_fusion.going, bf16[6144,1024]{1,0:T(8,128)(2,1)} %bitcast.21, bf16[6144,1024]{1,0:T(8,128)(2,1)} %bitcast.22, bf16[1024,6144]{1,0:T(8,128)(2,1)} %bitcast.23), custom_call_target="tpu_custom_call" | custom-call | flops 12079595520 | bytes 37748736 | tf_op jit(solution)/shard_map/expert_layer/pallas_call | solution.py:269
  84.7 0.0 copy-done.3
  84.7 1.6 %fusion.1.x_in = bf16[128,1536]{1,0:T(8,128)(2,1)S(1)} fusion(bf16[4,40,1536]{2,1,0:T(8,128)(2,1)} %expert_layer.1, bf16[128,1536]{1,0:T(8,128)(2,1)S(1)} %copy-done.3, f32[128]{0:T(128)S(1)} %get-tuple-element.4, s32[128]{0:T(128)S(1)} %get-tuple-element.7, f32[128]{0:T(128)S(1)} %get-tuple-element.5, s32[4,40]{1,0:T(4,128)S(1)} %multiply_add_fusion, ...), kind=kOutput, calls=%fused_computation.3 | convolution fusion | flops 378179584 | bytes 1280640 | tf_op jit(solution)/shard_map/iec,ecd->id/dot_general | solution.py:617
  86.3 0.0 copy-start.2
  86.4 1.7 %copy-done.2 = bf16[1536,768]{1,0:T(8,128)(2,1)S(1)} copy-done((bf16[1536,768]{1,0:T(8,128)(2,1)S(1)}, bf16[1536,768]{1,0:T(8,128)(2,1)}, u32[]{:S(2)}) %copy-start.2) | copy-done | bytes 2359320
  88.0 0.0 copy-start.1
  88.0 62.8 %attention_layer.1 = bf16[256,768]{1,0:T(8,128)(2,1)S(1)} custom-call(bf16[128,1536]{1,0:T(8,128)(2,1)S(1)} %fusion.1.x_in, f32[1,1536]{1,0:T(1,128)S(1)} %reshape.61.gain, bf16[1536,768]{1,0:T(8,128)(2,1)S(1)} %copy-done.2, bf16[1536,1024]{1,0:T(8,128)(2,1)} %wk_hbm.1, bf16[1536,1024]{1,0:T(8,128)(2,1)} %wv_hbm.1), custom_call_target="tpu_custom_call" | custom-call | flops 3623878656 | bytes 3538944 | tf_op jit(solution)/shard_map/attention_layer/pallas_call | solution.py:544
  150.8 0.7 copy.17
  151.6 0.0 copy-done.1
  (5 shorter events, 0.0 us)
Async XLA Ops:
  0.6 1.9 %copy-start = (f32[1536,4]{0,1:T(4,128)S(1)}, f32[1536,4]{0,1:T(4,128)}, u32[]{:S(2)}) copy-start(f32[1536,4]{0,1:T(4,128)} %param.15) | copy-start | bytes 73732
  16.1 68.5 %copy-start.3 = (bf16[128,1536]{1,0:T(8,128)(2,1)S(1)}, bf16[128,1536]{1,0:T(8,128)(2,1)}, u32[]{:S(2)}) copy-start(bf16[128,1536]{1,0:T(8,128)(2,1)} %param.12) | copy-start | bytes 1179652
  86.3 1.7 %copy-start.2 = (bf16[1536,768]{1,0:T(8,128)(2,1)S(1)}, bf16[1536,768]{1,0:T(8,128)(2,1)}, u32[]{:S(2)}) copy-start(bf16[1536,768]{1,0:T(8,128)(2,1)} %wq_hbm.1) | copy-start | bytes 7077892
  88.0 63.6 %copy-start.1 = (bf16[128,1536]{1,0:T(8,128)(2,1)}, bf16[128,1536]{1,0:T(8,128)(2,1)S(1)}, u32[]{:S(2)}) copy-start(bf16[128,1536]{1,0:T(8,128)(2,1)S(1)} %fusion.1.x_in) | copy-start | bytes 1179652

commit v4 on v3

--- a/solution.py
+++ b/solution.py
@@ -477,15 +477,28 @@
         q[i * tb : (i + 1) * tb, :] = value[:, :qw]
         kv[t, i * tb : (i + 1) * tb, :] = value[:, qw:]
 
+    nc, c, k = nt // 2, t // 2, t % 2
+    sib = (p, e, c * 2 + (1 - k))
+
+    def share(block, s_at, r_at, peer):
+        return copy(kv.at[block], kv.at[block], ks.at[s_at], kr.at[r_at], peer)
+
     shares = [
-        copy(kv.at[t], kv.at[t], ks.at[dt], kr.at[nt - dt], (p, e, lax.rem(t + dt, nt)))
-        for dt in range(1, nt)
+        share(t, 2 * far, 2 * (nc - far), (p, e, lax.rem(c + far, nc) * 2 + k))
+        for far in range(1, nc)
     ]
-    for share in shares:
-        share.start()
-    for dt in range(1, nt):
-        block = kv.at[lax.rem(t + dt, nt)]
-        copy(block, block, ks.at[dt], kr.at[dt], (p, e, lax.rem(t + dt, nt))).wait_recv()
+    shares.append(share(t, 1, 1, sib))
+    for one in shares:
+        one.start()
+    for far in range(1, nc):
+        block = lax.rem(c + far, nc) * 2 + k
+        share(block, 2 * far, 2 * far, sib).wait_recv()
+        relay = share(block, 2 * far + 1, 2 * far + 1, sib)
+        relay.start()
+        shares.append(relay)
+    for far in range(nc):
+        block = lax.rem(c + far, nc) * 2 + (1 - k)
+        share(block, 2 * far + 1, 2 * far + 1, sib).wait_recv()
 
     tokens = nt * qr
 
@@ -510,8 +523,8 @@
 
     lax.fori_loop(0, heads, one_head, 0)
 
-    for share in shares:
-        share.wait_send()
+    for one in shares:
+        one.wait_send()
     for s in range(ne):
         for d in range(2):
             if s:

time: 153 us -> 151 us (0.987)
  no operation moved by 1% of the time
where the time goes in v4:
time: 151 us
  Pallas kernels  131 us (87%)
  blocking collectives  8.33 us (6%)
  matrix products  5.49 us (4%)
  local copies, waits for them, and re-layouts  3.14 us (2%)
  other arithmetic  2.6 us (2%)
    pallas_call x1, Pallas kernels, expert_layer(): pl.pallas_call(functools.partial(expert_kernel, np_, ne, nt, going.shape)...  68.5 us
    pallas_call x1, Pallas kernels, attention_layer(): pl.pallas_call(functools.partial(attend_kernel, np_, ne, nt), out_shape=j...  62.1 us
    psum x1, blocking collectives, on_device(): squares, logit_sum = lax.psum((square_part, logit_part), 'tensor')  8.33 us

profile of v4, /device:TPU:0, one launch (start us, length us, event | category | flops | bytes accessed | tf_op | source)
XLA Modules:
  0.0 150.8 jit_solution(10461017916858658222)
XLA Ops:
  0.6 0.0 copy-start
  0.6 1.2 fusion.5
  1.8 0.7 compare_select_fusion
  2.5 0.0 copy-done
  2.5 1.7 %fusion.3 = f32[128,4]{0,1:T(4,128)S(1)} fusion(f32[1536,4]{0,1:T(4,128)S(1)} %copy-done, bf16[128,1536]{1,0:T(8,128)(2,1)} %param.12, f32[1536]{0:T(1024)} %param.13), kind=kOutput, calls=%fused_computation.7 | convolution fusion | flops 9830400 | bytes 425984 | tf_op jit(solution)/shard_map/dot_general | solution.py:609
  4.2 8.3 %all-reduce = (f32[128]{0:T(128)S(1)}, f32[128,4]{0,1:T(4,128)S(1)}) all-reduce(f32[128]{0:T(128)S(1)} %fusion.5, f32[128,4]{0,1:T(4,128)S(1)} %fusion.3), channel_id=1, replica_groups=mesh['pipe'=2,'expert'=4,'tensor'=4] {'tensor'}, use_global_device_ids=true, to_apply=%region_1.0 | all-reduce | flops 640 | bytes 5120 | tf_op jit(solution)/shard_map/psum | solution.py:610
  12.6 0.7 select_reduce_fusion
  13.3 0.7 reshape.61.gain
  14.0 2.1 %convolution_convert_fusion.going = bf16[4,40,1536]{2,1,0:T(8,128)(2,1)} fusion(bf16[128,1536]{1,0:T(8,128)(2,1)} %param.12, f32[128]{0:T(128)S(1)} %add_rsqrt_fusion, f32[1536]{0:T(1024)} %param.13, s32[128]{0:T(128)S(1)} %get-tuple-element.7, s32[4,40]{1,0:T(4,128)S(1)} %multiply_add_fusion, s32[128]{0:T(128)S(1)} %get-tuple-element.6), kind=kOutput, calls=%fused_computation.2 | convolution fusion | flops 64008192 | bytes 893056 | tf_op jit(solution)/shard_map/eci,id->ecd/dot_general | solution.py:622
  16.1 0.0 copy-start.3
  16.1 68.5 %expert_layer.1 = bf16[4,40,1536]{2,1,0:T(8,128)(2,1)} custom-call(bf16[4,40,1536]{2,1,0:T(8,128)(2,1)} %convolution_convert_fusion.going, bf16[6144,1024]{1,0:T(8,128)(2,1)} %bitcast.21, bf16[6144,1024]{1,0:T(8,128)(2,1)} %bitcast.22, bf16[1024,6144]{1,0:T(8,128)(2,1)} %bitcast.23), custom_call_target="tpu_custom_call" | custom-call | flops 12079595520 | bytes 37748736 | tf_op jit(solution)/shard_map/expert_layer/pallas_call | solution.py:269
  84.7 0.0 copy-done.3
  84.7 1.6 %fusion.1.x_in = bf16[128,1536]{1,0:T(8,128)(2,1)S(1)} fusion(bf16[4,40,1536]{2,1,0:T(8,128)(2,1)} %expert_layer.1, bf16[128,1536]{1,0:T(8,128)(2,1)S(1)} %copy-done.3, f32[128]{0:T(128)S(1)} %get-tuple-element.4, s32[128]{0:T(128)S(1)} %get-tuple-element.7, f32[128]{0:T(128)S(1)} %get-tuple-element.5, s32[4,40]{1,0:T(4,128)S(1)} %multiply_add_fusion, ...), kind=kOutput, calls=%fused_computation.3 | convolution fusion | flops 378179584 | bytes 1280640 | tf_op jit(solution)/shard_map/iec,ecd->id/dot_general | solution.py:630
  86.3 0.0 copy-start.2
  86.4 1.7 %copy-done.2 = bf16[1536,768]{1,0:T(8,128)(2,1)S(1)} copy-done((bf16[1536,768]{1,0:T(8,128)(2,1)S(1)}, bf16[1536,768]{1,0:T(8,128)(2,1)}, u32[]{:S(2)}) %copy-start.2) | copy-done | bytes 2359320
  88.0 0.0 copy-start.1
  88.0 62.1 %attention_layer.1 = bf16[256,768]{1,0:T(8,128)(2,1)S(1)} custom-call(bf16[128,1536]{1,0:T(8,128)(2,1)S(1)} %fusion.1.x_in, f32[1,1536]{1,0:T(1,128)S(1)} %reshape.61.gain, bf16[1536,768]{1,0:T(8,128)(2,1)S(1)} %copy-done.2, bf16[1536,1024]{1,0:T(8,128)(2,1)} %wk_hbm.1, bf16[1536,1024]{1,0:T(8,128)(2,1)} %wv_hbm.1), custom_call_target="tpu_custom_call" | custom-call | flops 3623878656 | bytes 3538944 | tf_op jit(solution)/shard_map/attention_layer/pallas_call | solution.py:557
  150.1 0.7 copy.17
  150.8 0.0 copy-done.1
  (5 shorter events, 0.0 us)
Async XLA Ops:
  0.6 1.9 %copy-start = (f32[1536,4]{0,1:T(4,128)S(1)}, f32[1536,4]{0,1:T(4,128)}, u32[]{:S(2)}) copy-start(f32[1536,4]{0,1:T(4,128)} %param.15) | copy-start | bytes 73732
  16.1 68.5 %copy-start.3 = (bf16[128,1536]{1,0:T(8,128)(2,1)S(1)}, bf16[128,1536]{1,0:T(8,128)(2,1)}, u32[]{:S(2)}) copy-start(bf16[128,1536]{1,0:T(8,128)(2,1)} %param.12) | copy-start | bytes 1179652
  86.3 1.7 %copy-start.2 = (bf16[1536,768]{1,0:T(8,128)(2,1)S(1)}, bf16[1536,768]{1,0:T(8,128)(2,1)}, u32[]{:S(2)}) copy-start(bf16[1536,768]{1,0:T(8,128)(2,1)} %wq_hbm.1) | copy-start | bytes 7077892
  88.0 62.8 %copy-start.1 = (bf16[128,1536]{1,0:T(8,128)(2,1)}, bf16[128,1536]{1,0:T(8,128)(2,1)S(1)}, u32[]{:S(2)}) copy-start(bf16[128,1536]{1,0:T(8,128)(2,1)S(1)} %fusion.1.x_in) | copy-start | bytes 1179652
